TPU v7x, 256 devices: a whole 4x4x8 slice. The times are simulated.
256 devices in a mesh: user: 32 (over y, z), hist: 8 (over x, core).
Axes of the slice: x: 4, y: 4, z: 8, core: 2. Of those that a mesh axis runs over, the one named last changes fastest.
Arguments:
- quot_ids: int32 [64, 2048], P('user', 'hist'), may hold values from 0 to 2047
- rem_ids: int32 [64, 2048], P('user', 'hist'), may hold values from 0 to 65535, as said below
- lengths: int32 [64], P('user'), may hold values from 426 to 2048, as said below
- log_decay: float32 [64, 4, 2048], P('user', None, 'hist'), may hold values from -1.1 to 0
- quot_table: bfloat16 [2048, 256], replicated, may hold values from -6 to 6
- rem_table: bfloat16 [65536, 256], P('user'), may hold values from -6 to 6
- w_query: bfloat16 [256, 256], replicated, may hold values from -0.375 to 0.375
- w_key: bfloat16 [256, 256], replicated, may hold values from -0.375 to 0.375
- w_value: bfloat16 [256, 256], replicated, may hold values from -0.375 to 0.375
- w_out: bfloat16 [256, 256], replicated, may hold values from -0.375 to 0.375
- cotangent: bfloat16 [64, 2048, 256], P('user', 'hist'), may hold values from -0.59765625 to 0.59765625
Outputs:
- output: bfloat16 [64, 2048, 256], P('user', 'hist')
- quot_grad: float32 [2048, 256], replicated
- rem_grad: float32 [65536, 256], P('user')
Inputs may be any that keep to these rules, and one draw needn't show every extreme that they name: rem_ids[u, t] // 2048 names a shard of the remainder table. In each aligned block of 256 events of one user (events b * 256 to (b + 1) * 256 - 1), no shard is named by more than 16 events, and one shard, the same for all blocks, is named by exactly 16. The valid events of user u are its first lengths[u] ones.
All inputs are finite; a program needn't handle non-finite values.
Results may differ from a plain program's by a relative error of at most 0.0073.
Values may be sent and summed in bfloat16 or wider, within the bound.
No kernel may reach another device: no remote copies, remote signals or barrier semaphores. Data moves between devices by JAX's collectives and lax.ppermute only.
A program may use at most 192 MiB of HBM per device.

v0:
```python
import math
import jax
import jax.numpy as jnp
from jax import lax
from jax.sharding import PartitionSpec as P

largest_value = lax.Precision.HIGHEST


def carried_in(part, axis, combine, identity):
    place = lax.axis_index(axis)
    gathered = jax.tree.map(lambda a: lax.all_gather(a, axis), part)
    state = jax.tree.map(lambda a, e: jnp.zeros_like(a) + jnp.asarray(e, a.dtype), part, identity)

    def one(step, state):
        return combine(
            state, jax.tree.map(lambda a: lax.dynamic_index_in_dim(a, step, 0, False), gathered)
        )

    return lax.fori_loop(0, place, one, state)


def carried_in_2(shard, axis, combine, identity):
    peers, place = (lax.axis_size(axis), lax.axis_index(axis))
    everything = jax.tree.map(
        lambda part, kind: lax.all_gather(part.astype(kind), axis),
        shard,
        (jnp.bfloat16, jnp.bfloat16),
    )
    start = jax.tree.map(
        lambda part, zero: jnp.broadcast_to(jnp.asarray(zero, part.dtype), part.shape),
        shard,
        identity,
    )

    def step(k, before):
        at = peers - 1 - k
        reached = at > place
        new = combine(
            before, jax.tree.map(lambda part, own: part[at].astype(own.dtype), everything, shard)
        )
        return jax.tree.map(lambda a, b: jnp.where(reached, a, b), new, before)

    return lax.fori_loop(0, peers, step, start)


def decay_mask(cumulative):
    length = cumulative.shape[-1]
    gap = cumulative[..., :, None] - cumulative[..., None, :]
    lower_tri = jnp.arange(length)[:, None] >= jnp.arange(length)[None, :]
    return jnp.where(lower_tri, jnp.exp(jnp.minimum(gap, 0.0)), 0.0)


def link_states(earlier, following):
    return (earlier[0] * following[0], following[0][..., None, None] * earlier[1] + following[1])


def body(
    quot_ids,
    rem_ids,
    lengths,
    log_decay,
    quot_table,
    rem_table,
    w_query,
    w_key,
    w_value,
    w_out,
    cotangent,
):
    user_count, block_len = quot_ids.shape
    feature_width = quot_table.shape[1]
    head_count = log_decay.shape[1]
    head_size = feature_width // head_count
    shards = lax.axis_size("user")
    hist_dev = lax.axis_size("hist")
    rows_own = rem_table.shape[0]
    capacity = 2 * block_len // shards
    history = block_len * hist_dev
    score_scale = 1.0 / math.sqrt(head_size * history)
    slot_total = float(user_count * shards * history)
    own_events = jnp.sum(lengths.astype(jnp.float32))
    all_events = lax.psum(own_events, "user")
    grad_ratio = slot_total / all_events
    flat_ids = rem_ids.reshape(-1)
    owners = flat_ids // rows_own
    matches = (
        owners.reshape(user_count, block_len)[..., None] == jnp.arange(shards, dtype=jnp.int32)
    ).astype(jnp.int32)
    before = jnp.cumsum(matches, axis=1) - matches
    ranking = jnp.sum(before * matches, axis=-1).reshape(-1)
    user_of = jnp.repeat(jnp.arange(user_count, dtype=jnp.int32), block_len)
    slot_index = (owners * user_count + user_of) * capacity + ranking
    requests = (
        jnp.full((shards * user_count * capacity,), -1, jnp.int32).at[slot_index].set(flat_ids)
    )
    requests = requests.reshape(shards, user_count * capacity)
    base_row = lax.axis_index("user") * rows_own
    wanted = lax.all_to_all(requests, "user", split_axis=0, concat_axis=0, tiled=True)
    present = wanted >= 0
    local_row = jnp.where(present, wanted - base_row, 0)
    found_rows = jnp.where(present[..., None], rem_table[local_row], jnp.zeros((), jnp.bfloat16))
    answered = lax.all_to_all(found_rows, "user", split_axis=0, concat_axis=0, tiled=True)
    rem_emb = answered.reshape(-1, feature_width)[slot_index]
    quot_emb = quot_table[quot_ids.reshape(-1)]
    embedded = (quot_emb.astype(jnp.float32) * rem_emb.astype(jnp.float32)).astype(jnp.bfloat16)

    def project(matrix):
        result = jnp.dot(embedded, matrix, preferred_element_type=jnp.float32).astype(jnp.bfloat16)
        return result.reshape(user_count, block_len, head_count, head_size)

    query_rows = project(w_query)
    key_rows = project(w_key)
    value_rows = project(w_value)
    cumulative = jnp.cumsum(log_decay, axis=-1)
    block_end = cumulative[..., -1]
    decay_all = jnp.exp(block_end)
    growth = jnp.exp(cumulative).transpose(0, 2, 1)[..., None]
    falloff = jnp.exp(block_end[..., None] - cumulative).transpose(0, 2, 1)[..., None]
    local_state = jnp.einsum(
        "ulhd,ulhe->uhde",
        key_rows.astype(jnp.float32) * falloff,
        value_rows.astype(jnp.float32),
        precision=largest_value,
    )
    entering = carried_in(
        (decay_all, local_state),
        "hist",
        link_states,
        (jnp.ones_like(decay_all), jnp.zeros_like(local_state)),
    )[1]

    def forward_user(inputs):
        single_query, single_key, single_value, cum_one, grow_one, state_one = inputs
        score_matrix = jnp.einsum(
            "tbc,xbc->btx", single_query, single_key, preferred_element_type=jnp.float32
        )
        weight_matrix = (score_scale * score_matrix * decay_mask(cum_one)).astype(jnp.bfloat16)
        within_bounds = jnp.einsum(
            "tov,vtp->otp", weight_matrix, single_value, preferred_element_type=jnp.float32
        )
        carried = score_scale * jnp.einsum(
            "lhd,hde->lhe",
            single_query.astype(jnp.float32) * grow_one,
            state_one,
            precision=largest_value,
        )
        return ((within_bounds + carried).astype(jnp.bfloat16), weight_matrix)

    mixed, weight_matrix = lax.map(
        forward_user, (query_rows, key_rows, value_rows, cumulative, growth, entering)
    )
    output = jnp.dot(
        mixed.reshape(-1, feature_width), w_out, preferred_element_type=jnp.float32
    ).astype(jnp.bfloat16)
    output = output.reshape(user_count, block_len, feature_width)
    position = lax.axis_index("hist") * block_len + jnp.arange(block_len, dtype=jnp.int32)
    in_history = position[None, :] < lengths[:, None]
    masked_cot = jnp.where(in_history[..., None], cotangent.astype(jnp.float32), 0.0).astype(
        jnp.bfloat16
    )
    dmixed = jnp.dot(
        masked_cot.reshape(-1, feature_width), w_out.T, preferred_element_type=jnp.float32
    ).astype(jnp.bfloat16)
    dmixed = dmixed.reshape(user_count, block_len, head_count, head_size)
    local_grad = jnp.einsum(
        "ulhd,ulhe->uhde",
        query_rows.astype(jnp.float32) * growth,
        dmixed.astype(jnp.float32),
        precision=largest_value,
    )
    leaving = carried_in_2(
        (decay_all, local_grad),
        "hist",
        link_states,
        (jnp.ones_like(decay_all), jnp.zeros_like(local_grad)),
    )[1]

    def backward_user(inputs):
        (
            single_query,
            single_key,
            single_value,
            dmixed_one,
            cum_one,
            grow_one,
            fall_one,
            weight_one,
            state_one,
            leaving_single,
        ) = inputs
        dscores = jnp.einsum(
            "lhe,mhe->hlm", dmixed_one, single_value, preferred_element_type=jnp.float32
        )
        weight_gradient = (score_scale * dscores * decay_mask(cum_one)).astype(jnp.bfloat16)
        dquery = jnp.einsum(
            "tov,vtp->otp", weight_gradient, single_key, preferred_element_type=jnp.float32
        ) + score_scale * grow_one * jnp.einsum(
            "hde,lhe->lhd", state_one, dmixed_one.astype(jnp.float32), precision=largest_value
        )
        dkeys = jnp.einsum(
            "euq,uex->qex", weight_gradient, single_query, preferred_element_type=jnp.float32
        ) + score_scale * fall_one * jnp.einsum(
            "kcg,wkg->wkc",
            leaving_single,
            single_value.astype(jnp.float32),
            precision=largest_value,
        )
        dvalue = jnp.einsum(
            "hlm,lhe->mhe", weight_one, dmixed_one, preferred_element_type=jnp.float32
        ) + score_scale * fall_one * jnp.einsum(
            "zxr,czx->czr", leaving_single, single_key.astype(jnp.float32), precision=largest_value
        )
        return (
            dquery.astype(jnp.bfloat16),
            dkeys.astype(jnp.bfloat16),
            dvalue.astype(jnp.bfloat16),
        )

    dquery, dkeys, dvalue = lax.map(
        backward_user,
        (
            query_rows,
            key_rows,
            value_rows,
            dmixed,
            cumulative,
            growth,
            falloff,
            weight_matrix,
            entering,
            leaving,
        ),
    )
    dembedded = jnp.dot(
        dquery.reshape(-1, feature_width), w_query.T, preferred_element_type=jnp.float32
    )
    dembedded = dembedded + jnp.dot(
        dkeys.reshape(-1, feature_width), w_key.T, preferred_element_type=jnp.float32
    )
    dembedded = dembedded + jnp.dot(
        dvalue.reshape(-1, feature_width), w_value.T, preferred_element_type=jnp.float32
    )
    quot_part = jax.ops.segment_sum(
        dembedded * rem_emb.astype(jnp.float32),
        quot_ids.reshape(-1),
        num_segments=quot_table.shape[0],
    )
    event_terms = dembedded * quot_emb.astype(jnp.float32)
    rem_send = (
        jnp.zeros((shards * user_count * capacity, feature_width), jnp.float32)
        .at[slot_index]
        .set(event_terms)
    )
    rem_send = rem_send.reshape(shards, user_count * capacity, feature_width)
    rem_back = lax.all_to_all(rem_send, "user", split_axis=0, concat_axis=0, tiled=True)
    present_ids = wanted >= 0
    local_rows = jnp.where(present_ids, wanted - base_row, 0).reshape(-1)
    rem_part = jax.ops.segment_sum(
        rem_back.reshape(-1, feature_width), local_rows, num_segments=rows_own
    )
    quot_part = grad_ratio * quot_part
    rem_part = grad_ratio * rem_part
    quot_grad = lax.psum(quot_part, ("user", "hist"))
    rem_grad = lax.psum(rem_part, "hist")
    return (output, quot_grad, rem_grad)


def solution(mesh):
    return jax.shard_map(
        body,
        mesh=mesh,
        in_specs=(
            P("user", "hist"),
            P("user", "hist"),
            P("user"),
            P("user", None, "hist"),
            P(),
            P("user", None),
            P(),
            P(),
            P(),
            P(),
            P("user", "hist", None),
        ),
        out_specs=(P("user", "hist", None), P(), P("user", None)),
        check_vma=False,
    )
```

profile of v0, /device:TPU:8, one launch (start us, length us, event | category | flops | bytes accessed | tf_op | source)
XLA Modules:
  0.0 589.0 jit_solution(10004334027409384725)
XLA Ops:
  9.4 1.2 reduce-window.14
  11.0 2.4 scatter_custom_fusion
  14.1 11.7 %all-to-all-start = ((s32[32,1,32]{2,1,0:T(1,128)}), s32[32,1,32]{2,1,0:T(1,128)S(1)}, u32[]{:S(2)}, u32[]{:S(2)}) async-start(s32[32,1,32]{2,1,0:T(1,128)} %all_to_all.12), calls=%async_computation | async-start | bytes 32768 | tf_op jit(solution)/shard_map/all_to_all | solution.py:99
  26.5 2.4 reduce-window.16
  30.3 4.1 all-to-all-done
  35.1 3.9 gather_fusion.1
  39.0 1.0 broadcast_select_fusion
  40.0 5.7 all-to-all-start.1
  45.9 10.6 %all-gather.3 = bf16[16,4,1]{1,2,0:T(2,128)(2,1)S(1)} all-gather(bf16[2,4,1]{1,2,0:T(2,128)(2,1)S(1)} %get-tuple-element.494), channel_id=5, replica_groups=mesh['user'=32,'hist'=8] {'hist'}, dimensions={0}, use_global_device_ids=true | all-gather | bytes 144 | tf_op jit(solution)/shard_map/all_gather | solution.py:26
  59.2 3.0 gather_fusion
  62.2 8.9 %all-gather = f32[16,4,1]{1,2,0:T(1,128)} all-gather(f32[2,4,1]{1,2,0:T(1,128)S(1)} %get-tuple-element.495), channel_id=2, replica_groups=mesh['user'=32,'hist'=8] {'hist'}, dimensions={0}, use_global_device_ids=true | all-gather | bytes 288 | tf_op jit(solution)/shard_map/all_gather | solution.py:12
  71.1 2.0 gather_fusion.2
  74.5 1.1 convolution_convert_fusion.2
  76.4 1.0 reshape.409
  77.5 1.7 convert_multiply_fusion.6
  79.2 1.1 convolution_convert_fusion.4
  80.3 1.0 reshape.489
  81.3 1.2 copy.95
  82.6 2.1 fusion.79
  85.1 14.8 %all-gather.2 = bf16[16,4,64,64]{3,2,1,0:T(8,128)(2,1)} all-gather(bf16[2,4,64,64]{3,2,1,0:T(8,128)(2,1)S(1)} %convolution_convert_fusion.5), channel_id=4, replica_groups=mesh['user'=32,'hist'=8] {'hist'}, dimensions={0}, use_global_device_ids=true | all-gather | bytes 589824 | tf_op jit(solution)/shard_map/all_gather | solution.py:26
  99.9 13.4 %while.57 = (s32[]{:T(128)}, f32[2,4,64,64]{3,2,1,0:T(8,128)S(1)}, s32[]{:T(128)}, bf16[8,2,4]{2,1,0:T(2,128)(2,1)}, bf16[8,2,4,64,64]{4,3,2,1,0:T(8,128)(2,1)},...) while((s32[]{:T(128)}, f32[2,4,64,64]{3,2,1,0:T(8,128)S(1)}, s32[]{:T(128)}, ...), condition=%wide.region_13.14_spmd.clone, body=%wide.region_12.13_spmd.clone.sunk | while | flops 163856 | bytes 327935 | solution.py:44
  100.6 1.0 fusion.168
  102.3 1.0 fusion.168
  104.0 1.0 fusion.168
  105.7 1.0 fusion.168
  107.4 1.0 fusion.168
  109.1 1.0 fusion.168
  110.7 1.0 fusion.168
  112.4 1.0 fusion.168
  113.7 4.2 while.55
  113.7 1.3 bitcast_dynamic-update-slice_fusion.2
  115.8 1.3 bitcast_dynamic-update-slice_fusion.2
  119.3 9.1 %while.56 = (s32[]{:T(128)}, bf16[2,256,4,64]{1,3,2,0:T(8,128)(2,1)}, bf16[2,256,4,64]{1,3,2,0:T(8,128)(2,1)S(1)}, bf16[2,256,4,64]{1,3,2,0:T(8,128)(2,1)S(1)}, ...) while((s32[]{:T(128)}, ...), condition=%wide.region_15.16_spmd, body=%wide.region_14.15_spmd.sunk | while | flops 287442944 | bytes 7786197 | solution.py:220
  120.7 1.3 fusion.167
  125.2 1.3 fusion.167
  128.8 1.2 copy.108
  131.3 3.5 scatter_custom_fusion.2
  134.8 9.8 %all-to-all-start.2 = ((f32[32,32,256]{2,1,0:T(8,128)}), f32[32,32,256]{2,1,0:T(8,128)}, u32[]{:S(2)}, u32[]{:S(2)}) async-start(f32[32,32,256]{2,1,0:T(8,128)} %bitcast.331), calls=%async_computation.2 | async-start | bytes 2097152 | tf_op jit(solution)/shard_map/all_to_all | solution.py:256
  145.3 79.2 %psum.21 = f32[]{:T(128)} all-reduce(f32[]{:T(128)} %convert_reduce_fusion), channel_id=1, replica_groups=mesh['user'=32,'hist'=8] {'user'}, use_global_device_ids=true, to_apply=%region_11.12 | all-reduce | flops 1 | bytes 8 | tf_op jit(solution)/shard_map/psum | solution.py:83
  225.1 4.3 scatter_custom_fusion.1
  229.5 1.5 broadcast_multiply_fusion.1
  231.7 7.0 %scatter_custom_fusion.3 = f32[2048,256]{1,0:T(8,128)S(1)} fusion(s32[1024]{0:T(1024)S(1)} %reshape.473, f32[1024,256]{1,0:T(8,128)} %bitcast.52, f32[]{:T(128)} %constant.162.clone.1), kind=kCustom, calls=%fused_computation.108 | custom fusion | flops 262144 | bytes 2097664 | tf_op jit(solution)/shard_map/scatter-add | solution.py:259
  238.8 1.5 broadcast_multiply_fusion
  241.5 1.0 convolution_convert_fusion.1
  242.5 262.9 %all-reduce.3.cloned.1.call-done = f32[2048,256]{1,0:T(8,128)} async-done(((f32[2048,256]{1,0:T(8,128)}), f32[2048,256]{1,0:T(8,128)}) %all-reduce.3.cloned.1.call-update) | async-done | bytes 2097168 | tf_op jit(solution)/shard_map/psum | solution.py:264
  505.4 72.6 %all-reduce.5.cloned.1.call-done = f32[2048,256]{1,0:T(8,128)} async-done(((f32[2048,256]{1,0:T(8,128)}), f32[2048,256]{1,0:T(8,128)}) %all-reduce.5.cloned.1.call-update) | async-done | bytes 2097168 | tf_op jit(solution)/shard_map/psum | solution.py:265
  578.0 3.2 copy.177
  581.2 1.3 copy.178
  (163 shorter events, 30.4 us)
Async XLA Ops:
  7.2 27.9 %copy-start = (bf16[2048,256]{1,0:T(8,128)(2,1)S(1)}, bf16[2048,256]{1,0:T(8,128)(2,1)}, u32[]{:S(2)}) copy-start(bf16[2048,256]{1,0:T(8,128)(2,1)} %param.24) | copy-start | bytes 3145732
  11.0 60.1 %copy-start.18 = (s32[512,1]{0,1:T(1,128)}, s32[512,1]{0,1:T(1,128)S(1)}, u32[]{:S(2)}) copy-start(s32[512,1]{0,1:T(1,128)S(1)} %compare_select_fusion.1) | copy-start | bytes 6148
  14.1 20.3 %all-to-all-start = ((s32[32,1,32]{2,1,0:T(1,128)}), s32[32,1,32]{2,1,0:T(1,128)S(1)}, u32[]{:S(2)}, u32[]{:S(2)}) async-start(s32[32,1,32]{2,1,0:T(1,128)} %all_to_all.12), calls=%async_computation | async-start | bytes 32768 | tf_op jit(solution)/shard_map/all_to_all | solution.py:99
  39.0 6.8 %copy-start.19 = (s32[2]{0:T(128)S(1)}, s32[2]{0:T(128)}, u32[]{:S(2)}) copy-start(s32[2]{0:T(128)} %param.21) | copy-start | bytes 28
  39.0 6.9 %copy-start.16 = (s32[2,256]{1,0:T(2,128)S(1)}, s32[2,256]{1,0:T(2,128)}, u32[]{:S(2)}) copy-start(s32[2,256]{1,0:T(2,128)} %param.19) | copy-start | bytes 6148
  39.0 19.2 %copy-start.14 = (bf16[2,256,256]{2,1,0:T(8,128)(2,1)S(1)}, bf16[2,256,256]{2,1,0:T(8,128)(2,1)}, u32[]{:S(2)}) copy-start(bf16[2,256,256]{2,1,0:T(8,128)(2,1)} %param.29) | copy-start | bytes 786436
  39.0 19.4 %copy-start.10 = (bf16[256,256]{1,0:T(8,128)(2,1)S(1)}, bf16[256,256]{1,0:T(8,128)(2,1)}, u32[]{:S(2)}) copy-start(bf16[256,256]{1,0:T(8,128)(2,1)} %param.28) | copy-start | bytes 393220
  40.0 31.0 %all-to-all-start.1 = ((bf16[32,32,256]{2,1,0:T(8,128)(2,1)}), bf16[32,32,256]{2,1,0:T(8,128)(2,1)S(1)}, u32[]{:S(2)}, u32[]{:S(2)}) async-start(bf16[32,32,256]{2,1,0:T(8,128)(2,1)} %broadcast_select_fusion), calls=%async_computation.1 | async-start | bytes 1048576 | tf_op jit(solution)/shard_map/all_to_all | solution.py:103
  45.8 67.6 %all-gather.6.cloned.1.call-start = ((), (), s32[]{:S(2)}) async-start(), calls=%async_computation.5 | async-start | bytes 2359296 | tf_op jit(solution)/shard_map/all_gather | solution.py:12
  59.2 13.9 %copy-start.9 = (bf16[256,256]{1,0:T(8,128)(2,1)S(1)}, bf16[256,256]{1,0:T(8,128)(2,1)}, u32[]{:S(2)}) copy-start(bf16[256,256]{1,0:T(8,128)(2,1)} %param.25) | copy-start | bytes 393220
  73.1 6.1 %copy-start.1 = (bf16[512,256]{1,0:T(8,128)(2,1)}, bf16[512,256]{1,0:T(8,128)(2,1)S(1)}, u32[]{:S(2)}) copy-start(bf16[512,256]{1,0:T(8,128)(2,1)S(1)} %gather_fusion.2) | copy-start | bytes 786436
  117.9 0.7 copy-start.7
  121.9 1.0 copy-start.5
  123.2 0.7 copy-start.6
  126.5 1.0 copy-start.5
  127.8 0.7 copy-start.6
  128.5 2.2 copy-start.12
  130.0 0.9 copy-start.13
  131.2 93.9 %copy-start.3 = (f32[512,256]{1,0:T(8,128)}, f32[512,256]{1,0:T(8,128)S(1)}, u32[]{:S(2)}) copy-start(f32[512,256]{1,0:T(8,128)S(1)} %convolution_add_fusion) | copy-start | bytes 1572868
  131.3 13.5 %copy-start.20 = (s32[2]{0:T(128)S(1)}, s32[2]{0:T(128)}, u32[]{:S(2)}) copy-start(s32[2]{0:T(128)} %param.21) | copy-start | bytes 28
  131.3 93.2 %copy-start.17 = (s32[2,256]{1,0:T(2,128)S(1)}, s32[2,256]{1,0:T(2,128)}, u32[]{:S(2)}) copy-start(s32[2,256]{1,0:T(2,128)} %param.19) | copy-start | bytes 6148
  131.3 93.8 %copy-start.2 = (bf16[512,256]{1,0:T(8,128)(2,1)S(1)}, bf16[512,256]{1,0:T(8,128)(2,1)}, u32[]{:S(2)}) copy-start(bf16[512,256]{1,0:T(8,128)(2,1)} %copy-done.1) | copy-start | bytes 786436
  134.8 96.9 %all-to-all-start.2 = ((f32[32,32,256]{2,1,0:T(8,128)}), f32[32,32,256]{2,1,0:T(8,128)}, u32[]{:S(2)}, u32[]{:S(2)}) async-start(f32[32,32,256]{2,1,0:T(8,128)} %bitcast.331), calls=%async_computation.2 | async-start | bytes 2097152 | tf_op jit(solution)/shard_map/all_to_all | solution.py:256
  144.7 360.8 %all-reduce.3.cloned.1.call-start = ((), (), s32[]{:S(2)}) async-start(), calls=%async_computation.3 | async-start | bytes 4194304 | tf_op jit(solution)/shard_map/psum | solution.py:264
  230.9 0.7 copy-start.15
  231.0 347.0 %all-reduce.5.cloned.1.call-start = ((), (), s32[]{:S(2)}) async-start(), calls=%async_computation.4 | async-start | bytes 4194304 | tf_op jit(solution)/shard_map/psum | solution.py:265
  240.2 0.9 copy-start.8
  240.2 1.3 copy-start.11
  578.0 3.2 copy-start.4
Sparse Core Ops, SparseCore 0:
  84.9 27.1 all-gather.5
  231.1 274.2 all-reduce.2
  508.4 69.5 all-reduce.4
where the time goes:
time: 591 us; the launch traced here: 589 us
  waiting for transfers between devices  340 us (58%)
  blocking collectives  113 us (19%)
  other arithmetic  42.9 us (7%)
  local copies, waits for them, and re-layouts  32.7 us (6%)
  starting transfers between devices  27.6 us (5%)
  matrix products  17.2 us (3%)
  between operations  14.9 us (3%)
    psum x1, waiting for transfers between devices, body(): quot_grad = lax.psum(quot_part, ('user', 'hist'))  263 us
    psum x1, blocking collectives, body(): all_events = lax.psum(own_events, 'user')  79.2 us
    psum x1, waiting for transfers between devices, body(): rem_grad = lax.psum(rem_part, 'hist')  72.6 us
    all_gather x2, blocking collectives, carried_in_2(): lax.all_gather(part.astype(kind), axis)  25.3 us
  transfers between devices with their start and end apart: 6, of which 3 were waited for; matrix products, arithmetic and copies ran while one was open for 7% of the time, Pallas kernels for 0%

commit v1 on v0

--- a/solution.py
+++ b/solution.py
@@ -3,6 +3,7 @@
 import jax.numpy as jnp
 from jax import lax
 from jax.sharding import PartitionSpec as P
+from jax.lax import psum
 
 largest_value = lax.Precision.HIGHEST
 
@@ -261,7 +262,8 @@
     )
     quot_part = grad_ratio * quot_part
     rem_part = grad_ratio * rem_part
-    quot_grad = lax.psum(quot_part, ("user", "hist"))
+    formed = psum(quot_part, "hist")
+    quot_grad = psum(formed, "user")
     rem_grad = lax.psum(rem_part, "hist")
     return (output, quot_grad, rem_grad)
 

time: 591 us -> 502 us (0.85)
  waiting for transfers between devices: 340 us -> 250 us
    psum x2, waiting for transfers between devices: 336 us -> 246 us  [the longest x1 155 us: body(): quot_grad = psum(formed, 'user')]
  transfers between devices with their start and end apart: 6 -> 6, of which waited for: 3 -> 3; matrix products, arithmetic and copies ran while one was open for 7% -> 6% of each run, Pallas kernels for 0% -> 0%
where the time goes in v1:
time: 502 us; the launch traced here: 499 us
  waiting for transfers between devices  250 us (50%)
  blocking collectives  113 us (23%)
  other arithmetic  43.2 us (9%)
  local copies, waits for them, and re-layouts  31.4 us (6%)
  starting transfers between devices  27.3 us (5%)
  matrix products  17.2 us (3%)
  between operations  15 us (3%)
    psum x1, waiting for transfers between devices, body(): quot_grad = psum(formed, 'user')  155 us
    psum x1, waiting for transfers between devices, body(): formed = psum(quot_part, 'hist')  91.1 us
    psum x1, blocking collectives, body(): all_events = lax.psum(own_events, 'user')  79.2 us
    all_gather x2, blocking collectives, carried_in_2(): lax.all_gather(part.astype(kind), axis)  25.3 us
    all_to_all x1, starting transfers between devices, body(): lax.all_to_all(requests, 'user', split_axis=0, concat_axis=0, tiled=True)  11.7 us
  transfers between devices with their start and end apart: 6, of which 3 were waited for; matrix products, arithmetic and copies ran while one was open for 6% of the time, Pallas kernels for 0%

profile of v1, /device:TPU:8, one launch (start us, length us, event | category | flops | bytes accessed | tf_op | source)
XLA Modules:
  0.0 498.6 jit_solution(9446364104226246527)
XLA Ops:
  9.4 1.2 reduce-window.14
  11.0 2.4 scatter_custom_fusion
  14.1 11.7 %all-to-all-start = ((s32[32,1,32]{2,1,0:T(1,128)}), s32[32,1,32]{2,1,0:T(1,128)S(1)}, u32[]{:S(2)}, u32[]{:S(2)}) async-start(s32[32,1,32]{2,1,0:T(1,128)} %all_to_all.12), calls=%async_computation | async-start | bytes 32768 | tf_op jit(solution)/shard_map/all_to_all | solution.py:100
  26.5 2.4 reduce-window.16
  30.3 4.1 all-to-all-done
  35.1 3.9 gather_fusion.1
  39.0 1.0 broadcast_select_fusion
  40.0 5.7 %all-to-all-start.1 = ((bf16[32,32,256]{2,1,0:T(8,128)(2,1)}), bf16[32,32,256]{2,1,0:T(8,128)(2,1)S(1)}, u32[]{:S(2)}, u32[]{:S(2)}) async-start(bf16[32,32,256]{2,1,0:T(8,128)(2,1)} %broadcast_select_fusion), calls=%async_computation.1 | async-start | bytes 1048576 | tf_op jit(solution)/shard_map/all_to_all | solution.py:104
  45.9 10.6 %all-gather.3 = bf16[16,4,1]{1,2,0:T(2,128)(2,1)S(1)} all-gather(bf16[2,4,1]{1,2,0:T(2,128)(2,1)S(1)} %get-tuple-element.496), channel_id=5, replica_groups=mesh['user'=32,'hist'=8] {'hist'}, dimensions={0}, use_global_device_ids=true | all-gather | bytes 144 | tf_op jit(solution)/shard_map/all_gather | solution.py:27
  59.2 3.0 gather_fusion
  62.2 8.9 %all-gather = f32[16,4,1]{1,2,0:T(1,128)} all-gather(f32[2,4,1]{1,2,0:T(1,128)S(1)} %get-tuple-element.497), channel_id=2, replica_groups=mesh['user'=32,'hist'=8] {'hist'}, dimensions={0}, use_global_device_ids=true | all-gather | bytes 288 | tf_op jit(solution)/shard_map/all_gather | solution.py:13
  71.1 2.0 gather_fusion.2
  74.4 1.1 convolution_convert_fusion.2
  76.4 1.0 reshape.409
  77.5 1.7 convert_multiply_fusion.6
  79.1 1.1 convolution_convert_fusion.4
  80.3 1.0 reshape.489
  81.3 1.2 copy.95
  82.6 2.1 fusion.79
  85.1 14.8 %all-gather.2 = bf16[16,4,64,64]{3,2,1,0:T(8,128)(2,1)} all-gather(bf16[2,4,64,64]{3,2,1,0:T(8,128)(2,1)S(1)} %convolution_convert_fusion.5), channel_id=4, replica_groups=mesh['user'=32,'hist'=8] {'hist'}, dimensions={0}, use_global_device_ids=true | all-gather | bytes 589824 | tf_op jit(solution)/shard_map/all_gather | solution.py:27
  99.9 13.5 %while.57 = (s32[]{:T(128)}, f32[2,4,64,64]{3,2,1,0:T(8,128)S(1)}, s32[]{:T(128)}, bf16[8,2,4]{2,1,0:T(2,128)(2,1)}, bf16[8,2,4,64,64]{4,3,2,1,0:T(8,128)(2,1)},...) while((s32[]{:T(128)}, f32[2,4,64,64]{3,2,1,0:T(8,128)S(1)}, s32[]{:T(128)}, ...), condition=%wide.region_13.14_spmd.clone, body=%wide.region_12.13_spmd.clone.sunk | while | flops 163856 | bytes 327935 | solution.py:45
  100.6 1.0 fusion.168
  102.3 1.0 fusion.168
  103.9 1.0 fusion.168
  105.7 1.0 fusion.168
  107.3 1.0 fusion.168
  109.1 1.0 fusion.168
  110.8 1.0 fusion.168
  112.4 1.0 fusion.168
  113.7 4.2 while.55
  113.8 1.3 bitcast_dynamic-update-slice_fusion.2
  115.9 1.3 bitcast_dynamic-update-slice_fusion.2
  119.4 9.1 %while.56 = (s32[]{:T(128)}, bf16[2,256,4,64]{1,3,2,0:T(8,128)(2,1)}, bf16[2,256,4,64]{1,3,2,0:T(8,128)(2,1)S(1)}, bf16[2,256,4,64]{1,3,2,0:T(8,128)(2,1)S(1)}, ...) while((s32[]{:T(128)}, ...), condition=%wide.region_15.16_spmd, body=%wide.region_14.15_spmd.sunk | while | flops 287442944 | bytes 7786197 | solution.py:221
  120.7 1.3 fusion.167
  125.3 1.3 fusion.167
  128.9 1.2 copy.108
  131.4 3.5 scatter_custom_fusion.2
  134.9 9.8 %all-to-all-start.2 = ((f32[32,32,256]{2,1,0:T(8,128)}), f32[32,32,256]{2,1,0:T(8,128)}, u32[]{:S(2)}, u32[]{:S(2)}) async-start(f32[32,32,256]{2,1,0:T(8,128)} %bitcast.331), calls=%async_computation.2 | async-start | bytes 2097152 | tf_op jit(solution)/shard_map/all_to_all | solution.py:257
  145.4 79.2 %psum.28 = f32[]{:T(128)} all-reduce(f32[]{:T(128)} %convert_reduce_fusion), channel_id=1, replica_groups=mesh['user'=32,'hist'=8] {'user'}, use_global_device_ids=true, to_apply=%region_11.12 | all-reduce | flops 1 | bytes 8 | tf_op jit(solution)/shard_map/psum | solution.py:84
  225.4 4.6 scatter_custom_fusion.1
  230.0 1.5 broadcast_multiply_fusion.1
  231.4 7.0 %scatter_custom_fusion.3 = f32[2048,256]{1,0:T(8,128)S(1)} fusion(s32[1024]{0:T(1024)S(1)} %reshape.473, f32[1024,256]{1,0:T(8,128)} %bitcast.52, f32[]{:T(128)} %constant.162.clone.1), kind=kCustom, calls=%fused_computation.108 | custom fusion | flops 262144 | bytes 2097664 | tf_op jit(solution)/shard_map/scatter-add | solution.py:260
  238.5 1.5 broadcast_multiply_fusion
  240.0 91.1 %all-reduce.6.cloned.1.call-done = (f32[2048,256]{1,0:T(8,128)}, f32[2048,256]{1,0:T(8,128)}) async-done(((f32[2048,256]{1,0:T(8,128)}, f32[2048,256]{1,0:T(8,128)}), (f32[2048,256]{1,0:T(8,128)}, f32[2048,256]{1,0:T(8,128)})) %all-reduce.6.cloned.1.call-update) | async-done | bytes 4194320 | tf_op jit(solution)/shard_map/psum | solution.py:265
  331.5 1.0 convolution_convert_fusion.1
  332.4 155.1 %all-reduce.4.cloned.1.call-done = f32[2048,256]{1,0:T(8,128)} async-done(((f32[2048,256]{1,0:T(8,128)}), f32[2048,256]{1,0:T(8,128)}) %all-reduce.4.cloned.1.call-update) | async-done | bytes 2097168 | tf_op jit(solution)/shard_map/psum | solution.py:266
  487.6 3.2 copy.178
  490.8 1.3 copy.179
  (163 shorter events, 29.0 us)
Async XLA Ops:
  7.2 27.9 %copy-start = (bf16[2048,256]{1,0:T(8,128)(2,1)S(1)}, bf16[2048,256]{1,0:T(8,128)(2,1)}, u32[]{:S(2)}) copy-start(bf16[2048,256]{1,0:T(8,128)(2,1)} %param.24) | copy-start | bytes 3145732
  11.0 60.1 %copy-start.18 = (s32[512,1]{0,1:T(1,128)}, s32[512,1]{0,1:T(1,128)S(1)}, u32[]{:S(2)}) copy-start(s32[512,1]{0,1:T(1,128)S(1)} %compare_select_fusion.1) | copy-start | bytes 6148
  14.1 20.3 %all-to-all-start = ((s32[32,1,32]{2,1,0:T(1,128)}), s32[32,1,32]{2,1,0:T(1,128)S(1)}, u32[]{:S(2)}, u32[]{:S(2)}) async-start(s32[32,1,32]{2,1,0:T(1,128)} %all_to_all.12), calls=%async_computation | async-start | bytes 32768 | tf_op jit(solution)/shard_map/all_to_all | solution.py:100
  39.0 6.8 %copy-start.19 = (s32[2]{0:T(128)S(1)}, s32[2]{0:T(128)}, u32[]{:S(2)}) copy-start(s32[2]{0:T(128)} %param.21) | copy-start | bytes 28
  39.0 6.9 %copy-start.16 = (s32[2,256]{1,0:T(2,128)S(1)}, s32[2,256]{1,0:T(2,128)}, u32[]{:S(2)}) copy-start(s32[2,256]{1,0:T(2,128)} %param.19) | copy-start | bytes 6148
  39.0 19.2 %copy-start.14 = (bf16[2,256,256]{2,1,0:T(8,128)(2,1)S(1)}, bf16[2,256,256]{2,1,0:T(8,128)(2,1)}, u32[]{:S(2)}) copy-start(bf16[2,256,256]{2,1,0:T(8,128)(2,1)} %param.29) | copy-start | bytes 786436
  39.0 19.3 %copy-start.10 = (bf16[256,256]{1,0:T(8,128)(2,1)S(1)}, bf16[256,256]{1,0:T(8,128)(2,1)}, u32[]{:S(2)}) copy-start(bf16[256,256]{1,0:T(8,128)(2,1)} %param.28) | copy-start | bytes 393220
  40.0 31.0 %all-to-all-start.1 = ((bf16[32,32,256]{2,1,0:T(8,128)(2,1)}), bf16[32,32,256]{2,1,0:T(8,128)(2,1)S(1)}, u32[]{:S(2)}, u32[]{:S(2)}) async-start(bf16[32,32,256]{2,1,0:T(8,128)(2,1)} %broadcast_select_fusion), calls=%async_computation.1 | async-start | bytes 1048576 | tf_op jit(solution)/shard_map/all_to_all | solution.py:104
  45.7 67.7 %all-gather.6.cloned.1.call-start = ((), (), s32[]{:S(2)}) async-start(), calls=%async_computation.4 | async-start | bytes 2359296 | tf_op jit(solution)/shard_map/all_gather | solution.py:13
  59.2 13.9 %copy-start.9 = (bf16[256,256]{1,0:T(8,128)(2,1)S(1)}, bf16[256,256]{1,0:T(8,128)(2,1)}, u32[]{:S(2)}) copy-start(bf16[256,256]{1,0:T(8,128)(2,1)} %param.25) | copy-start | bytes 393220
  73.0 6.1 %copy-start.1 = (bf16[512,256]{1,0:T(8,128)(2,1)}, bf16[512,256]{1,0:T(8,128)(2,1)S(1)}, u32[]{:S(2)}) copy-start(bf16[512,256]{1,0:T(8,128)(2,1)S(1)} %gather_fusion.2) | copy-start | bytes 786436
  117.9 0.7 copy-start.7
  122.0 1.0 copy-start.5
  123.3 0.7 copy-start.6
  126.6 1.0 copy-start.5
  127.9 0.7 copy-start.6
  128.6 2.2 copy-start.12
  130.1 0.9 copy-start.13
  131.3 94.1 %copy-start.3 = (f32[512,256]{1,0:T(8,128)}, f32[512,256]{1,0:T(8,128)S(1)}, u32[]{:S(2)}) copy-start(f32[512,256]{1,0:T(8,128)S(1)} %convolution_add_fusion) | copy-start | bytes 1572868
  131.3 13.4 %copy-start.20 = (s32[2]{0:T(128)S(1)}, s32[2]{0:T(128)}, u32[]{:S(2)}) copy-start(s32[2]{0:T(128)} %param.21) | copy-start | bytes 28
  131.3 93.3 %copy-start.17 = (s32[2,256]{1,0:T(2,128)S(1)}, s32[2,256]{1,0:T(2,128)}, u32[]{:S(2)}) copy-start(s32[2,256]{1,0:T(2,128)} %param.19) | copy-start | bytes 6148
  131.3 94.0 %copy-start.15 = (s32[32,1,32]{2,0,1:T(8,128)S(1)}, s32[32,1,32]{2,0,1:T(8,128)}, u32[]{:S(2)}) copy-start(s32[32,1,32]{2,0,1:T(8,128)} %get-tuple-element.487) | copy-start | bytes 12292
  131.4 94.0 %copy-start.2 = (bf16[512,256]{1,0:T(8,128)(2,1)S(1)}, bf16[512,256]{1,0:T(8,128)(2,1)}, u32[]{:S(2)}) copy-start(bf16[512,256]{1,0:T(8,128)(2,1)} %copy-done.1) | copy-start | bytes 786436
  134.9 96.5 %all-to-all-start.2 = ((f32[32,32,256]{2,1,0:T(8,128)}), f32[32,32,256]{2,1,0:T(8,128)}, u32[]{:S(2)}, u32[]{:S(2)}) async-start(f32[32,32,256]{2,1,0:T(8,128)} %bitcast.331), calls=%async_computation.2 | async-start | bytes 2097152 | tf_op jit(solution)/shard_map/all_to_all | solution.py:257
  144.7 186.4 %all-reduce.6.cloned.1.call-start = ((), (), s32[]{:S(2)}) async-start(), calls=%async_computation.5 | async-start | bytes 8388608 | tf_op jit(solution)/shard_map/psum | solution.py:265
  240.0 91.2 %copy-start.8 = (bf16[2,256,4,64]{1,3,2,0:T(8,128)(2,1)S(1)}, bf16[2,256,4,64]{1,3,2,0:T(8,128)(2,1)}, u32[]{:S(2)}) copy-start(bf16[2,256,4,64]{1,3,2,0:T(8,128)(2,1)} %copy-done.7) | copy-start | bytes 786436
  240.0 91.5 %copy-start.11 = (bf16[256,256]{1,0:T(8,128)(2,1)S(1)}, bf16[256,256]{1,0:T(8,128)(2,1)}, u32[]{:S(2)}) copy-start(bf16[256,256]{1,0:T(8,128)(2,1)} %param.28) | copy-start | bytes 393220
  240.0 247.6 %all-reduce.4.cloned.1.call-start = ((), (), s32[]{:S(2)}) async-start(), calls=%async_computation.3 | async-start | bytes 4194304 | tf_op jit(solution)/shard_map/psum | solution.py:266
  487.6 3.2 copy-start.4
Sparse Core Ops, SparseCore 0:
  84.9 27.3 all-gather.5
  240.1 90.9 all-reduce.5
  334.6 152.8 all-reduce.3
